TPU v7x, 256 devices: a whole 4x4x8 slice. The times are simulated.
256 devices in a mesh: grp: 16 (over x, z_hi, core), sp: 16 (over y, z_lo).
Axes of the slice: x: 4, y: 4, z: 8 (z_hi: 2, z_lo: 4; z = z_hi * 4 + z_lo), core: 2. Of those that a mesh axis runs over, the one named last changes fastest.
Arguments:
- video: bfloat16 [16, 16, 128, 128, 128], P('grp', None, None, 'sp'), may hold values from -12 to 12
- cache: bfloat16 [16, 2, 128, 128, 128], P('grp', None, None, 'sp'), may hold values from -6 to 6
- conv_weight: bfloat16 [128, 3456], replicated, may hold values from -0.109375 to 0.109375
- latent_weight: bfloat16 [16, 128], replicated, may hold values from -0.5 to 0.5
- clip_lengths: int32 [16], replicated, may hold values from 1 to 16, as said below
Outputs:
- latents: bfloat16 [16, 16, 16, 128, 128], P('grp', None, None, 'sp')
Inputs may be any that keep to these rules, and one draw needn't show every extreme that they name: `clip_lengths`: some clip has all 16 frames live and some clip a single one.
All inputs are finite; a program needn't handle non-finite values.
Results may differ from a plain program's by a relative error of at most 0.002.
Values may be sent and summed in bfloat16 or wider, within the bound.
No kernel may reach another device: no remote copies, remote signals or barrier semaphores. Data moves between devices by JAX's collectives and lax.ppermute only.
A program may use at most 128 MiB of HBM per device.

v0:
```python
import jax
import jax.numpy as jnp
from jax import lax
from jax.sharding import PartitionSpec as P

NORM_GROUPS = 32


epsilon = 1e-06


def with_halo(shard, sides, width):
    for axis, dim in sides:
        count, length = (lax.axis_size(axis), shard.shape[dim])
        up = [(i, (i + 1) % count) for i in range(count - 1)]
        down = [(j, i) for i, j in up]
        last = lax.slice_in_dim(shard, length - width, length, axis=dim)
        leading = lax.slice_in_dim(shard, 0, width, axis=dim)
        before = lax.ppermute(last, axis, up)
        after = lax.ppermute(leading, axis, down)
        shard = jnp.concatenate([before, shard, after], axis=dim)
    return shard


def unfold(window, height, width):
    pieces = []
    for depth in range(3):
        for down in range(3):
            for across in range(3):
                pieces.append(window[depth, :, down : down + height, across : across + width])
    stacked = jnp.stack(pieces, 0)
    return stacked.reshape(27 * window.shape[1], height * width)


def conv_latent(window, own_frame, conv_weight, latent_f32, height, width):
    widened = jnp.pad(window, ((0, 0), (0, 0), (0, 0), (1, 1)))
    columns = unfold(widened, height, width)
    conv_out = jnp.dot(conv_weight, columns, preferred_element_type=jnp.float32)
    own = own_frame.astype(jnp.float32).reshape(own_frame.shape[0], height * width)
    mixed = jax.nn.silu(own + conv_out)
    return jnp.dot(latent_f32, mixed, precision=lax.Precision.HIGHEST)


def body(video, cache, conv_weight, latent_weight, clip_lengths):
    clip = video[0]
    prior = cache[0]
    frames, chans, height, width = clip.shape
    latent_n = latent_weight.shape[0]
    strips = lax.axis_size("sp")
    group_index = lax.axis_index("grp")
    table = jnp.arange(clip_lengths.shape[0], dtype=jnp.int32)
    length = jnp.sum(jnp.where(table == group_index, clip_lengths, 0))
    positions = jnp.arange(frames, dtype=jnp.int32)
    live_mask = (positions < length).astype(jnp.float32)
    per_group = chans // NORM_GROUPS
    grouped = clip.astype(jnp.float32).reshape(frames, NORM_GROUPS, per_group, height, width)
    weights = live_mask[:, None, None, None, None]
    part_sums = jnp.sum(grouped * weights, axis=(0, 2, 3, 4))
    part_squares = jnp.sum(grouped * grouped * weights, axis=(0, 2, 3, 4))
    sums, squares = lax.psum((part_sums, part_squares), "sp")
    count = length.astype(jnp.float32) * (per_group * height * strips * width)
    group_mean = sums / count
    variance = squares / count - group_mean * group_mean
    inverse = lax.rsqrt(variance + epsilon)
    normed = (grouped - group_mean[None, :, None, None, None]) * inverse[None, :, None, None, None]
    activated = jax.nn.silu(normed).reshape(frames, chans, height, width).astype(jnp.bfloat16)
    sequence = jnp.concatenate([prior, activated], 0)
    rimmed = with_halo(sequence, (("sp", 2),), 1)
    latent_f32 = latent_weight.astype(jnp.float32)
    empty = jnp.zeros((latent_n, height * width), jnp.float32)

    def compute(items):
        return conv_latent(items[0], items[1], conv_weight, latent_f32, height, width)

    def skipped(items):
        return empty

    source_frame = (positions - group_index) % frames
    triples = jnp.stack([jnp.take(rimmed, source_frame + offset, axis=0) for offset in range(3)], 1)
    frames_sent = jnp.take(clip, source_frame, axis=0)
    flags = (source_frame < length).astype(jnp.int32)
    arrived, arrived_frames, arrived_flags = (
        lax.all_to_all(triples, "grp", split_axis=0, concat_axis=0, tiled=True),
        lax.all_to_all(frames_sent, "grp", split_axis=0, concat_axis=0, tiled=True),
        lax.all_to_all(flags, "grp", split_axis=0, concat_axis=0, tiled=True),
    )

    def one_item(items):
        return lax.cond(items[2] > 0, compute, skipped, (items[0], items[1]))

    computed = lax.map(one_item, (arrived, arrived_frames, arrived_flags))
    returned = lax.all_to_all(
        computed.astype(jnp.bfloat16), "grp", split_axis=0, concat_axis=0, tiled=True
    ).astype(computed.dtype)
    latent = jnp.take(returned, (positions + group_index) % frames, axis=0)
    latent = latent * live_mask[:, None, None]
    return latent.astype(jnp.bfloat16).reshape(1, frames, latent_n, height, width)


def solution(mesh):
    in_specs = (P("grp", None, None, "sp", None), P("grp", None, None, "sp", None), P(), P(), P())
    out_specs = P("grp", None, None, "sp", None)
    return jax.shard_map(body, mesh=mesh, in_specs=in_specs, out_specs=out_specs, check_vma=False)
```

profile of v0, /device:TPU:33, one launch (start us, length us, event | category | flops | bytes accessed | tf_op | source)
XLA Modules:
  0.0 829.7 jit_solution(16433476367827460424)
XLA Ops:
  2.7 10.7 %all-to-all-start = ((s32[16,1,1]{2,1,0:T(1,128)}), s32[16,1,1]{2,1,0:T(1,128)S(1)}, u32[]{:S(2)}, u32[]{:S(2)}) async-start(s32[16,1,1]{2,1,0:T(1,128)} %compare_convert_fusion), calls=%async_computation | async-start | bytes 16384 | tf_op jit(solution)/shard_map/all_to_all | solution.py:85
  19.7 32.1 %all-reduce.1 = (f32[32]{0:T(128)S(1)}, f32[32]{0:T(128)S(1)}) all-reduce(f32[32]{0:T(128)S(1)} %reduce_sum.44, f32[32]{0:T(128)S(1)} %reduce_sum.47), channel_id=1, replica_groups=mesh['grp'=16,'sp'=16] {'sp'}, use_global_device_ids=true, to_apply=%region_3.4 | all-reduce | flops 64 | bytes 512 | tf_op jit(solution)/shard_map/psum | solution.py:60
  68.1 16.5 %all-to-all-start.1 = ((bf16[16,128,8,128]{3,2,1,0:T(8,128)(2,1)}), bf16[16,128,8,128]{3,2,1,0:T(8,128)(2,1)}, u32[]{:S(2)}, u32[]{:S(2)}) async-start(bf16[16,128,8,128]{3,2,1,0:T(8,128)(2,1)} %broadcast_select_fusion), calls=%async_computation.1 | async-start | bytes 8388608 | tf_op jit(solution)/shard_map/all_to_all | solution.py:84
  98.3 97.2 %collective-permute-done = bf16[18,128,1,128]{3,1,2,0:T(8,128)(2,1)S(1)} collective-permute-done((bf16[18,128,1,128]{3,1,2,0:T(8,128)(2,1)S(1)}, bf16[18,128,1,128]{3,1,2,0:T(8,128)(2,1)S(1)}, u32[]{:S(2)}, u32[]{:S(2)}) %collective-permute-start) | collective-permute-done | bytes 589856 | tf_op jit(solution)/shard_map/ppermute | solution.py:19
  199.6 7.9 pad_maximum_fusion.1
  207.5 8.5 %gather_fusion.4 = bf16[16,128,10,128]{3,2,1,0:T(8,128)(2,1)} fusion(bf16[18,128,10,128]{3,2,1,0:T(8,128)(2,1)} %pad_maximum_fusion.1, s32[1024]{0:T(1024)S(1)} %pad_clamp_fusion.1), kind=kCustom, calls=%fused_computation.2.clone | custom fusion | bytes 10485824 | tf_op jit(solution)/shard_map/jit(_take)/gather | solution.py:79
  215.9 8.5 %gather_fusion.2 = bf16[16,128,10,128]{3,2,1,0:T(8,128)(2,1)} fusion(bf16[18,128,10,128]{3,2,1,0:T(8,128)(2,1)} %pad_maximum_fusion.1, s32[1024]{0:T(1024)S(1)} %pad_clamp_fusion.3), kind=kCustom, calls=%fused_computation.clone | custom fusion | bytes 10485824 | tf_op jit(solution)/shard_map/jit(_take)/gather | solution.py:79
  224.5 8.5 %gather_fusion.3 = bf16[16,128,10,128]{3,2,1,0:T(8,128)(2,1)} fusion(bf16[18,128,10,128]{3,2,1,0:T(8,128)(2,1)} %pad_maximum_fusion.1, s32[1024]{0:T(1024)S(1)} %pad_clamp_fusion.2), kind=kCustom, calls=%fused_computation.1.clone | custom fusion | bytes 10485824 | tf_op jit(solution)/shard_map/jit(_take)/gather | solution.py:79
  255.6 13.6 %pad_maximum_fusion = bf16[16,3,128,10,128]{4,3,2,0,1:T(8,128)(2,1)S(1)} fusion(bf16[16,1,128,10,128]{4,3,2,0,1:T(8,128)(2,1)} %select_bitcast_fusion, bf16[16,1,128,10,128]{4,3,2,0,1:T(8,128)(2,1)} %select_bitcast_fusion.1, bf16[16,1,128,10,128]{4,3,2,0,1:T(8,128)(2,1)} %select_bitcast_fusion.2), kind=kLoop, calls=%fused_computation.66 | loop fusion | flops 15728640 | bytes 31457280 | tf_op jit(solution)/shard_map/stack | solution.py:79
  269.2 8.1 copy.19
  277.3 10.7 %all-to-all-start.2 = ((bf16[16,3,128,10,128]{4,2,3,1,0:T(8,128)(2,1)}), bf16[16,3,128,10,128]{4,2,3,1,0:T(8,128)(2,1)}, u32[]{:S(2)}, u32[]{:S(2)}) async-start(bf16[16,3,128,10,128]{4,2,3,1,0:T(8,128)(2,1)} %copy.19), calls=%async_computation.2 | async-start | bytes 31457280 | tf_op jit(solution)/shard_map/all_to_all | solution.py:83
  295.2 338.9 %all-to-all-done.2 = bf16[16,3,128,10,128]{4,2,3,1,0:T(8,128)(2,1)} async-done(((bf16[16,3,128,10,128]{4,2,3,1,0:T(8,128)(2,1)}), bf16[16,3,128,10,128]{4,2,3,1,0:T(8,128)(2,1)}, u32[]{:S(2)}, u32[]{:S(2)}) %all-to-all-start.2) | async-done | bytes 15728672 | tf_op jit(solution)/shard_map/all_to_all | solution.py:83
  634.1 22.6 %copy.21 = bf16[16,3,128,10,128]{4,3,2,1,0:T(8,128)(2,1)} copy(bf16[16,3,128,10,128]{4,2,3,1,0:T(8,128)(2,1)} %all-to-all-done.2) | data formatting | bytes 31457280 | tf_op jit(solution)/shard_map/while | solution.py:91
  656.7 109.6 %while.10 = (s32[]{:T(128)}, bf16[16,16,1024]{2,1,0:T(8,128)(2,1)}, s32[16]{0:T(128)S(1)}, bf16[16,128,8,128]{1,3,2,0:T(8,128)(2,1)}, bf16[16,3,128,10,128]{4,3,...) while((s32[]{:T(128)}, bf16[16,16,1024]{2,1,0:T(8,128)(2,1)}, ...), condition=%wide.region_10.12_spmd, body=%wide.region_7.11_spmd.sunk | while | flops 931921920 | bytes 49029808 | solution.py:91
  658.0 9.9 %conditional.2 = (bf16[1,16,1024]{2,1,0:T(8,128)(2,1)S(1)}) conditional(s32[]{:T(128)} %bitcast.42, () %tuple.42, (bf16[16,128,8,128]{1,3,2,0:T(8,128)(2,1)}, s32[]{:T(128)}, bf16[16,3,128,10,128]{4,3,2,1,0:T(8,128)(2,1)}, bf16[128,3456]{1,0:T(8,128)(2,1)S(1)}, f32[16,128]{1,0:T(8,128)S(1)}) %tuple.43), branch_computations={%region_8.9_spmd, %region_9.10_spmd} | conditional | flops 931921920 | bytes 48963600 | solution.py:89
  669.8 9.9 %conditional.2 = (bf16[1,16,1024]{2,1,0:T(8,128)(2,1)S(1)}) conditional(s32[]{:T(128)} %bitcast.42, () %tuple.42, (bf16[16,128,8,128]{1,3,2,0:T(8,128)(2,1)}, s32[]{:T(128)}, bf16[16,3,128,10,128]{4,3,2,1,0:T(8,128)(2,1)}, bf16[128,3456]{1,0:T(8,128)(2,1)S(1)}, f32[16,128]{1,0:T(8,128)S(1)}) %tuple.43), branch_computations={%region_8.9_spmd, %region_9.10_spmd} | conditional | flops 931921920 | bytes 48963600 | solution.py:89
  687.3 9.9 %conditional.2 = (bf16[1,16,1024]{2,1,0:T(8,128)(2,1)S(1)}) conditional(s32[]{:T(128)} %bitcast.42, () %tuple.42, (bf16[16,128,8,128]{1,3,2,0:T(8,128)(2,1)}, s32[]{:T(128)}, bf16[16,3,128,10,128]{4,3,2,1,0:T(8,128)(2,1)}, bf16[128,3456]{1,0:T(8,128)(2,1)S(1)}, f32[16,128]{1,0:T(8,128)S(1)}) %tuple.43), branch_computations={%region_8.9_spmd, %region_9.10_spmd} | conditional | flops 931921920 | bytes 48963600 | solution.py:89
  699.1 9.9 %conditional.2 = (bf16[1,16,1024]{2,1,0:T(8,128)(2,1)S(1)}) conditional(s32[]{:T(128)} %bitcast.42, () %tuple.42, (bf16[16,128,8,128]{1,3,2,0:T(8,128)(2,1)}, s32[]{:T(128)}, bf16[16,3,128,10,128]{4,3,2,1,0:T(8,128)(2,1)}, bf16[128,3456]{1,0:T(8,128)(2,1)S(1)}, f32[16,128]{1,0:T(8,128)S(1)}) %tuple.43), branch_computations={%region_8.9_spmd, %region_9.10_spmd} | conditional | flops 931921920 | bytes 48963600 | solution.py:89
  716.7 9.9 %conditional.2 = (bf16[1,16,1024]{2,1,0:T(8,128)(2,1)S(1)}) conditional(s32[]{:T(128)} %bitcast.42, () %tuple.42, (bf16[16,128,8,128]{1,3,2,0:T(8,128)(2,1)}, s32[]{:T(128)}, bf16[16,3,128,10,128]{4,3,2,1,0:T(8,128)(2,1)}, bf16[128,3456]{1,0:T(8,128)(2,1)S(1)}, f32[16,128]{1,0:T(8,128)S(1)}) %tuple.43), branch_computations={%region_8.9_spmd, %region_9.10_spmd} | conditional | flops 931921920 | bytes 48963600 | solution.py:89
  730.4 9.9 %conditional.2 = (bf16[1,16,1024]{2,1,0:T(8,128)(2,1)S(1)}) conditional(s32[]{:T(128)} %bitcast.42, () %tuple.42, (bf16[16,128,8,128]{1,3,2,0:T(8,128)(2,1)}, s32[]{:T(128)}, bf16[16,3,128,10,128]{4,3,2,1,0:T(8,128)(2,1)}, bf16[128,3456]{1,0:T(8,128)(2,1)S(1)}, f32[16,128]{1,0:T(8,128)S(1)}) %tuple.43), branch_computations={%region_8.9_spmd, %region_9.10_spmd} | conditional | flops 931921920 | bytes 48963600 | solution.py:89
  744.1 9.9 %conditional.2 = (bf16[1,16,1024]{2,1,0:T(8,128)(2,1)S(1)}) conditional(s32[]{:T(128)} %bitcast.42, () %tuple.42, (bf16[16,128,8,128]{1,3,2,0:T(8,128)(2,1)}, s32[]{:T(128)}, bf16[16,3,128,10,128]{4,3,2,1,0:T(8,128)(2,1)}, bf16[128,3456]{1,0:T(8,128)(2,1)S(1)}, f32[16,128]{1,0:T(8,128)S(1)}) %tuple.43), branch_computations={%region_8.9_spmd, %region_9.10_spmd} | conditional | flops 931921920 | bytes 48963600 | solution.py:89
  755.8 9.9 %conditional.2 = (bf16[1,16,1024]{2,1,0:T(8,128)(2,1)S(1)}) conditional(s32[]{:T(128)} %bitcast.42, () %tuple.42, (bf16[16,128,8,128]{1,3,2,0:T(8,128)(2,1)}, s32[]{:T(128)}, bf16[16,3,128,10,128]{4,3,2,1,0:T(8,128)(2,1)}, bf16[128,3456]{1,0:T(8,128)(2,1)S(1)}, f32[16,128]{1,0:T(8,128)S(1)}) %tuple.43), branch_computations={%region_8.9_spmd, %region_9.10_spmd} | conditional | flops 931921920 | bytes 48963600 | solution.py:89
  766.4 41.5 %all-to-all-start.3 = ((bf16[16,16,1024]{2,1,0:T(8,128)(2,1)}), bf16[16,16,1024]{2,1,0:T(8,128)(2,1)S(1)}, u32[]{:S(2)}, u32[]{:S(2)}) async-start(bf16[16,16,1024]{2,1,0:T(8,128)(2,1)} %get-tuple-element.93), calls=%async_computation.3 | async-start | bytes 1048576 | tf_op jit(solution)/shard_map/all_to_all | solution.py:92
  807.9 19.7 %all-to-all-done.3 = bf16[16,16,1024]{2,1,0:T(8,128)(2,1)S(1)} async-done(((bf16[16,16,1024]{2,1,0:T(8,128)(2,1)}), bf16[16,16,1024]{2,1,0:T(8,128)(2,1)S(1)}, u32[]{:S(2)}, u32[]{:S(2)}) %all-to-all-start.3) | async-done | bytes 524320 | tf_op jit(solution)/shard_map/all_to_all | solution.py:92
  (359 shorter events, 172.7 us)
Async XLA Ops:
  2.7 65.4 %all-to-all-start = ((s32[16,1,1]{2,1,0:T(1,128)}), s32[16,1,1]{2,1,0:T(1,128)S(1)}, u32[]{:S(2)}, u32[]{:S(2)}) async-start(s32[16,1,1]{2,1,0:T(1,128)} %compare_convert_fusion), calls=%async_computation | async-start | bytes 16384 | tf_op jit(solution)/shard_map/all_to_all | solution.py:85
  14.1 5.2 copy-start.3
  63.3 21.3 %copy-start.1 = (bf16[1,2,128,8,128]{4,3,2,1,0:T(8,128)(2,1)S(1)}, bf16[1,2,128,8,128]{4,3,2,1,0:T(8,128)(2,1)}, u32[]{:S(2)}) copy-start(bf16[1,2,128,8,128]{4,3,2,1,0:T(8,128)(2,1)} %param.12) | copy-start | bytes 1572868
  68.1 209.2 %all-to-all-start.1 = ((bf16[16,128,8,128]{3,2,1,0:T(8,128)(2,1)}), bf16[16,128,8,128]{3,2,1,0:T(8,128)(2,1)}, u32[]{:S(2)}, u32[]{:S(2)}) async-start(bf16[16,128,8,128]{3,2,1,0:T(8,128)(2,1)} %broadcast_select_fusion), calls=%async_computation.1 | async-start | bytes 8388608 | tf_op jit(solution)/shard_map/all_to_all | solution.py:84
  84.6 114.9 %copy-start = (bf16[16,128,8,128]{3,2,1,0:T(8,128)(2,1)S(1)}, bf16[16,128,8,128]{3,2,1,0:T(8,128)(2,1)}, u32[]{:S(2)}) copy-start(bf16[16,128,8,128]{3,2,1,0:T(8,128)(2,1)} %multiply_convert_fusion) | copy-start | bytes 12582916
  90.0 105.4 %collective-permute-start = (bf16[18,128,1,128]{3,1,2,0:T(8,128)(2,1)S(1)}, bf16[18,128,1,128]{3,1,2,0:T(8,128)(2,1)S(1)}, u32[]{:S(2)}, u32[]{:S(2)}) collective-permute-start(bf16[18,128,1,128]{3,1,2,0:T(8,128)(2,1)S(1)} %copy.15), channel_id=1, source_target_pairs={{0,1},{1,2},{2,3},{3,4},{4,5},{5,6},{6,7},{7,8},{8,9},{9,10},{10,1... | collective-permute-start | bytes 1769480 | tf_op jit(solution)/shard_map/ppermute | solution.py:19
  92.2 106.3 %collective-permute-start.1 = (bf16[18,128,1,128]{3,1,2,0:T(8,128)(2,1)S(1)}, bf16[18,128,1,128]{3,1,2,0:T(8,128)(2,1)S(1)}, u32[]{:S(2)}, u32[]{:S(2)}) collective-permute-start(bf16[18,128,1,128]{3,1,2,0:T(8,128)(2,1)S(1)} %copy.16), channel_id=1, source_target_pairs={{1,0},{2,1},{3,2},{4,3},{5,4},{6,5},{7,6},{8,7},{9,8},{10,9},{11,1... | collective-permute-start | bytes 1769480 | tf_op jit(solution)/shard_map/ppermute | solution.py:20
  277.3 10.7 %copy-start.2 = (bf16[16,128]{1,0:T(8,128)(2,1)S(1)}, bf16[16,128]{1,0:T(8,128)(2,1)}, u32[]{:S(2)}) copy-start(bf16[16,128]{1,0:T(8,128)(2,1)} %param.14) | copy-start | bytes 12292
  277.3 356.8 %all-to-all-start.2 = ((bf16[16,3,128,10,128]{4,2,3,1,0:T(8,128)(2,1)}), bf16[16,3,128,10,128]{4,2,3,1,0:T(8,128)(2,1)}, u32[]{:S(2)}, u32[]{:S(2)}) async-start(bf16[16,3,128,10,128]{4,2,3,1,0:T(8,128)(2,1)} %copy.19), calls=%async_computation.2 | async-start | bytes 31457280 | tf_op jit(solution)/shard_map/all_to_all | solution.py:83
  295.2 361.5 %copy-start.6 = (bf16[128,3456]{1,0:T(8,128)(2,1)S(1)}, bf16[128,3456]{1,0:T(8,128)(2,1)}, u32[]{:S(2)}) copy-start(bf16[128,3456]{1,0:T(8,128)(2,1)} %param.13) | copy-start | bytes 2654212
  656.7 171.9 %copy-start.4 = (f32[16]{0:T(128)S(1)}, f32[16]{0:T(128)}, u32[]{:S(2)}) copy-start(f32[16]{0:T(128)} %copy-done.3) | copy-start | bytes 196
  656.7 171.9 %copy-start.5 = (pred[16]{0:T(512)(128)(4,1)S(1)}, pred[16]{0:T(512)(128)(4,1)}, u32[]{:S(2)}) copy-start(pred[16]{0:T(512)(128)(4,1)} %get-tuple-element.142) | copy-start | bytes 52
  766.4 61.3 %all-to-all-start.3 = ((bf16[16,16,1024]{2,1,0:T(8,128)(2,1)}), bf16[16,16,1024]{2,1,0:T(8,128)(2,1)S(1)}, u32[]{:S(2)}, u32[]{:S(2)}) async-start(bf16[16,16,1024]{2,1,0:T(8,128)(2,1)} %get-tuple-element.93), calls=%async_computation.3 | async-start | bytes 1048576 | tf_op jit(solution)/shard_map/all_to_all | solution.py:92
where the time goes:
time: 832 us; the launch traced here: 830 us
  waiting for transfers between devices  458 us (55%)
  local copies, waits for them, and re-layouts  149 us (18%)
  starting transfers between devices  87 us (10%)
  other arithmetic  70.1 us (8%)
  blocking collectives  32.1 us (4%)
  matrix products  21.9 us (3%)
  loops' own time  11.2 us (1%)
    all_to_all x1, waiting for transfers between devices, body(): lax.all_to_all(triples, 'grp', split_axis=0, concat_axis=0, tiled=True)  339 us
    ppermute x1, waiting for transfers between devices, with_halo(): before = lax.ppermute(last, axis, up)  97.2 us
    all_to_all x1, starting transfers between devices, body(): lax.all_to_all(computed.astype(jnp.bfloat16), 'grp', split_axis=0, concat...  41.5 us
    another operation x4, other arithmetic, body(): jnp.stack([jnp.take(rimmed, source_frame + offset, axis=0) for offset in...  36.2 us
    cond x208, local copies, waits for them, and re-layouts  33.3 us
    psum x1, blocking collectives, body(): sums, squares = lax.psum((part_sums, part_squares), 'sp')  32.1 us
    while x2, local copies, waits for them, and re-layouts, body(): computed = lax.map(one_item, (arrived, arrived_frames, arrived_flags))  29.4 us
    gather x3, local copies, waits for them, and re-layouts, body(): jnp.take(rimmed, source_frame + offset, axis=0)  25.5 us
  transfers between devices with their start and end apart: 6, of which 4 were waited for; matrix products, arithmetic and copies ran while one was open for 14% of the time, Pallas kernels for 0%

commit v1 on v0

v1 whole, which is shorter than its diff:
```python
import functools

import jax
import jax.numpy as jnp
from jax import lax
from jax.experimental import pallas as pl
from jax.experimental.pallas import tpu as pltpu
from jax.sharding import PartitionSpec as P

NORM_GROUPS = 32
epsilon = 1e-06
F32 = jnp.float32
BF16 = jnp.bfloat16


def half_silu(u):
    return u + u * jnp.tanh(u)


def stage_kernel(
    lengths_ref, video_ref, cache_ref, first_out_ref, last_out_ref, stats_ref,
    held_ref, rows_ref, acc_ref, first_ref, last_ref, sems, out_sems,
):
    total, chans, width = first_ref.shape
    height = video_ref.shape[1] // chans
    per_group = chans // NORM_GROUPS
    part = 16
    length = lengths_ref[lax.axis_index("grp")]

    def fetch(p):
        return pltpu.make_async_copy(video_ref.at[pl.ds(2 * p - 2, 2)], held_ref.at[pl.ds(2 * p, 2)], sems.at[p])

    def fetch_cache():
        return pltpu.make_async_copy(cache_ref, held_ref.at[pl.ds(0, 2)], sems.at[0])

    def leave(p, part):
        held, out = ((first_ref, first_out_ref), (last_ref, last_out_ref))[part]
        return pltpu.make_async_copy(held.at[pl.ds(2 * p, 2)], out.at[pl.ds(2 * p, 2)], out_sems.at[p, part])

    for p in range(1, total // 2):
        fetch(p).start()
    fetch_cache().start()
    acc_ref[...] = jnp.zeros_like(acc_ref)

    def turn(j, t, live):
        for k in range(chans // part):
            rows = slice(k * part * height, (k + 1) * part * height)
            x = held_ref[t, rows].astype(F32)
            rows_ref[j, rows] = x
            if live is not None:
                some = slice(k * part // per_group, (k + 1) * part // per_group)
                grouped = x.reshape(part // per_group, per_group, height, width)
                acc_ref[0, some] += jnp.sum(grouped, axis=1) * live
                acc_ref[1, some] += jnp.sum(grouped * grouped, axis=1) * live
        first_ref[t] = rows_ref[j, pl.ds(0, chans, stride=height), :].astype(BF16)
        last_ref[t] = rows_ref[j, pl.ds(height - 1, chans, stride=height), :].astype(BF16)

    def pair(p, carry):
        fetch(p).wait()
        for j in range(2):
            turn(j, 2 * p + j, (2 * p - 2 + j < length).astype(F32))
        for part in range(2):
            leave(p, part).start()
        return carry

    lax.fori_loop(1, total // 2, pair, 0)
    fetch_cache().wait()
    for j in range(2):
        turn(j, j, None)
    for part in range(2):
        leave(0, part).start()
    partial = jnp.sum(acc_ref[...], axis=2).reshape(2 * NORM_GROUPS, width)
    stats_ref[...] = lax.dot_general(
        jnp.ones((stats_ref.shape[0], width), F32), partial, (((1,), (1,)), ((), ())),
        precision=lax.Precision.HIGHEST, preferred_element_type=F32,
    )
    for p in range(total // 2):
        for part in range(2):
            leave(p, part).wait()


def stage(lengths, video, cache, chans, copies):
    frames, rows, width = video.shape
    total = frames + 2
    vmem = pl.BlockSpec(memory_space=pltpu.VMEM)
    hbm = pl.BlockSpec(memory_space=pl.ANY)
    return pl.pallas_call(
        stage_kernel,
        in_specs=[pl.BlockSpec(memory_space=pltpu.SMEM), hbm, hbm],
        out_specs=[hbm, hbm, vmem],
        out_shape=[
            pltpu.HBM((total, chans, width), BF16),
            pltpu.HBM((total, chans, width), BF16),
            jax.ShapeDtypeStruct((copies, 2 * NORM_GROUPS), F32),
        ],
        scratch_shapes=[
            pltpu.VMEM((total, rows, width), BF16),
            pltpu.VMEM((2, rows, width), F32),
            pltpu.VMEM((2, NORM_GROUPS, rows // chans, width), F32),
            pltpu.VMEM((total, chans, width), BF16),
            pltpu.VMEM((total, chans, width), BF16),
            pltpu.SemaphoreType.DMA((total // 2,)),
            pltpu.SemaphoreType.DMA((total // 2, 2)),
        ],
        compiler_params=pltpu.CompilerParams(vmem_limit_bytes=20 * 1024 * 1024),
        cost_estimate=pl.CostEstimate(flops=10_000_000, bytes_accessed=5_000_000, transcendentals=0),
    )(lengths, in_hbm(video), in_hbm(cache))


def in_hbm(value):
    return pltpu.with_memory_space_constraint(value, pltpu.HBM)


def prepare_kernel(first_in_ref, last_in_ref, raw_ref, first_ref, last_ref, weight_ref):
    chans = raw_ref.shape[0]
    for b in range(3):
        for a in range(3):
            for e in range(3):
                source = ((a * 3 + b) * 3 + e) * chans
                column = (b * 3 + a) * chans
                weight_ref[e * chans : (e + 1) * chans, column : column + chans] = raw_ref[:, source : source + chans]


def prepare(first, last, weight):
    chans = weight.shape[0]
    vmem = pl.BlockSpec(memory_space=pltpu.VMEM)
    hbm = pl.BlockSpec(memory_space=pl.ANY)
    return pl.pallas_call(
        prepare_kernel,
        in_specs=[hbm, hbm, vmem],
        out_specs=[hbm, hbm, vmem],
        out_shape=[
            pltpu.HBM(first.shape, BF16),
            pltpu.HBM(last.shape, BF16),
            jax.ShapeDtypeStruct((3 * chans, 9 * chans), BF16),
        ],
        input_output_aliases={0: 0, 1: 1},
        compiler_params=pltpu.CompilerParams(vmem_limit_bytes=16 * 1024 * 1024),
        cost_estimate=pl.CostEstimate(flops=6_000_000_000, bytes_accessed=20_000_000, transcendentals=0),
    )(in_hbm(first), in_hbm(last), weight)


def fill_norm(stats_ref, lengths_ref, norm_ref):
    _, chans, width = norm_ref.shape
    strips, groups2 = stats_ref.shape
    per_group = chans // NORM_GROUPS
    height = 8
    count = (lengths_ref[lax.axis_index("grp")] * (per_group * height * strips * width)).astype(F32)
    row = jnp.sum(stats_ref[...], axis=0, keepdims=True) * jnp.ones((chans, 1), F32) / count
    lane = lax.broadcasted_iota(jnp.int32, (chans, groups2), 1)
    group = lax.broadcasted_iota(jnp.int32, (chans, groups2), 0) // per_group
    mean = jnp.sum(jnp.where(lane == group, row, 0.0), axis=1, keepdims=True)
    square = jnp.sum(jnp.where(lane == group + NORM_GROUPS, row, 0.0), axis=1, keepdims=True)
    scale = 0.5 * lax.rsqrt(square - mean * mean + epsilon)
    norm_ref[0] = jnp.broadcast_to(scale, (chans, width))
    norm_ref[1] = jnp.broadcast_to(-mean * scale, (chans, width))


def shift_sum(y, chans, width):
    outs = []
    lane = lax.broadcasted_iota(jnp.int32, (chans, width), 1)
    for f in range(y.shape[1] // width):
        part = slice(f * width, (f + 1) * width)
        left = pltpu.roll(y[0:chans, part], 1, 1)
        right = pltpu.roll(y[2 * chans : 3 * chans, part], width - 1, 1)
        outs.append(
            y[chans : 2 * chans, part] + jnp.where(lane > 0, left, 0.0) + jnp.where(lane < width - 1, right, 0.0)
        )
    return outs


def project(latent, mixed):
    latent2 = jnp.concatenate([latent, latent], axis=1)
    value = jnp.concatenate(mixed, axis=1)
    high = value.astype(BF16)
    low = (value - high.astype(F32)).astype(BF16)
    return jnp.dot(latent2, jnp.concatenate([high, low], axis=0), preferred_element_type=F32)


def conv_kernel(
    lengths_ref, stats_ref, video_ref, cache_ref, weight_ref, latent_ref, lat_ref, edge_ref,
    seq_ref, rows_ref, norm_ref, sems, *buffers,
):
    pair, height, chans, width = buffers[0].shape
    total = seq_ref.shape[0]
    pairs = total // 2
    held, owns = buffers[:3], buffers[3:]
    deep = 3 * chans
    order = [list(range(1, 4)), list(range(4, 7)), [0], [height - 1]]

    def fetch(p):
        return pltpu.make_async_copy(video_ref.at[pl.ds(2 * p - 2, 2)], seq_ref.at[pl.ds(2 * p, 2)], sems.at[p])

    def fetch_cache():
        return pltpu.make_async_copy(cache_ref, seq_ref.at[pl.ds(0, 2)], sems.at[0])

    fetch_cache().start()
    for p in range(1, pairs):
        fetch(p).start()
    fill_norm(stats_ref, lengths_ref, norm_ref)

    def widen(p):
        for j in range(pair):
            rows_ref[j] = seq_ref[2 * p + j].astype(F32)

    def turn(j, r):
        return rows_ref[j, pl.ds(r, chans, stride=height), :]

    def activate(k, r):
        for j in range(pair):
            x = turn(j, r)
            owns[k % 3][j, r] = x.astype(BF16)
            held[k % 3][j, r] = half_silu(x * norm_ref[0] + norm_ref[1]).astype(BF16)

    fetch_cache().wait()
    widen(0)
    for r in range(height):
        for j in range(pair):
            held[0][j, r] = turn(j, r).astype(BF16)
    fetch(1).wait()
    widen(1)
    for r in range(height):
        activate(1, r)

    def taps_of(r):
        return [b for b in range(3) if 0 <= r + b - 1 < height]

    def step(p, k, more):
        before, now, own_ref = held[(k - 1) % 3], held[k % 3], owns[k % 3]
        if more:
            fetch(p + 1).wait()
            widen(p + 1)

        def multiply(rows):
            taps = taps_of(rows[0])
            columns = []
            for r in rows:
                for f in range(pair):
                    blocks = []
                    for b in taps:
                        for a in range(3):
                            source = before if f + a < 2 else now
                            blocks.append(source[(f + a) % 2, r + b - 1])
                    columns.append(jnp.concatenate(blocks, axis=0))
            x = jnp.concatenate(columns, axis=1)
            return jnp.dot(weight_ref[:, taps[0] * deep : (taps[-1] + 1) * deep], x, preferred_element_type=F32)

        def mix(rows, y):
            conv = shift_sum(y, chans, width)
            places = [(r, f) for r in rows for f in range(pair)]
            mixed = [conv[i] + own_ref[f, r].astype(F32) for i, (r, f) in enumerate(places)]
            if rows[0] == 0 or rows[0] == height - 1:
                for m, (r, f) in zip(mixed, places):
                    edge_ref[2 * p - 2 + f, 0 if r == 0 else 1] = m
                return None
            return [half_silu(0.5 * m) for m in mixed]

        def write(rows, mixed):
            latent = project(latent_ref[...], mixed)
            places = [(r, f) for r in rows for f in range(pair)]
            for i, (r, f) in enumerate(places):
                lat_ref[2 * p - 2 + f, pl.ds(r, latent.shape[0], stride=height), :] = latent[:, i * width : (i + 1) * width]

        to_mix, to_write = [], []
        to_activate = list(range(height)) if more else []
        for rows in order:
            y = multiply(rows)
            if to_mix:
                done, its = to_mix.pop(0)
                mixed = mix(done, its)
                if mixed is not None:
                    to_write.append((done, mixed))
            for _ in range(-(-height // len(order))):
                if to_activate:
                    activate(k + 1, to_activate.pop(0))
            if len(to_write) > 1:
                write(*to_write.pop(0))
            to_mix.append((rows, y))
        for done, its in to_mix:
            mixed = mix(done, its)
            if mixed is not None:
                to_write.append((done, mixed))
        for item in to_write:
            write(*item)

    def steps(i, carry):
        for k in range(1, 4):
            step(3 * i + k, k, True)
        return carry

    turns = (pairs - 2) // 3
    lax.fori_loop(0, turns, steps, 0)
    for p in range(3 * turns + 1, pairs):
        step(p, p, p + 1 < pairs)


def convolve(lengths, stats, video, cache, weight, latent):
    frames, rows, width = video.shape
    chans = weight.shape[0] // 3
    height = rows // chans
    total = frames + 2
    lat = latent.shape[0]
    vmem = pl.BlockSpec(memory_space=pltpu.VMEM)
    hbm = pl.BlockSpec(memory_space=pl.ANY)
    return pl.pallas_call(
        conv_kernel,
        in_specs=[pl.BlockSpec(memory_space=pltpu.SMEM), vmem, hbm, hbm, vmem, vmem],
        out_specs=[vmem, vmem],
        out_shape=[
            jax.ShapeDtypeStruct((frames, lat * height, width), F32),
            jax.ShapeDtypeStruct((frames, 2, chans, width), F32),
        ],
        scratch_shapes=[
            pltpu.VMEM((total, rows, width), BF16),
            pltpu.VMEM((2, rows, width), F32),
            pltpu.VMEM((2, chans, width), F32),
            pltpu.SemaphoreType.DMA((total // 2,)),
        ]
        + [pltpu.VMEM((2, height, chans, width), BF16)] * 6,
        compiler_params=pltpu.CompilerParams(vmem_limit_bytes=24 * 1024 * 1024),
        cost_estimate=pl.CostEstimate(flops=13_000_000_000, bytes_accessed=14_000_000, transcendentals=4_000_000),
    )(lengths, stats, in_hbm(video), in_hbm(cache), weight, latent)


def finish_kernel(
    side, final, lengths_ref, stats_ref, row_ref, weight_ref, latent_ref, lat_ref, edge_ref, out_ref,
    norm_ref, halo_ref, *scratch,
):
    total, chans, width = row_ref.shape
    frames = total - 2
    lat = latent_ref.shape[0]
    height = lat_ref.shape[1] // lat
    deep = 3 * chans
    length = lengths_ref[lax.axis_index("grp")]
    strip = lax.axis_index("sp")
    inside = (strip < lax.axis_size("sp") - 1 if side else strip > 0).astype(F32)
    fill_norm(stats_ref, lengths_ref, norm_ref)

    def activate(t):
        value = row_ref[t].astype(F32)
        if t >= 2:
            value = half_silu(value * norm_ref[0] + norm_ref[1])
        halo_ref[t] = (value * inside).astype(BF16)

    def multiply(p):
        columns = [jnp.concatenate([halo_ref[2 * p + f + a] for a in range(3)], axis=0) for f in range(2)]
        return jnp.dot(
            weight_ref[:, 2 * side * deep : (2 * side + 1) * deep], jnp.concatenate(columns, axis=1), preferred_element_type=F32
        )

    def mix(p, y):
        conv = shift_sum(y, chans, width)
        return [half_silu(0.5 * (conv[f] + edge_ref[2 * p + f, side])) for f in range(2)]

    def write(p, mixed):
        latent = project(latent_ref[...], mixed)
        rows_ref = scratch[0] if final else out_ref
        for f in range(2):
            t = 2 * p + f
            rows_ref[t, pl.ds(side * (height - 1), lat, stride=height), :] = latent[:, f * width : (f + 1) * width]
            if final:
                live = (t < length).astype(F32)
                out_ref[t] = (rows_ref[t] * live).reshape(lat, height, width).astype(BF16)

    if final:
        scratch[0][...] = lat_ref[...]
    else:
        out_ref[...] = lat_ref[...]
    for t in range(4):
        activate(t)
    to_mix, to_write = [], []
    for p in range(frames // 2):
        y = multiply(p)
        for t in (2 * p + 4, 2 * p + 5):
            if t < total:
                activate(t)
        if to_mix:
            before = to_mix.pop(0)
            to_write.append((before[0], mix(*before)))
        if len(to_write) > 1:
            write(*to_write.pop(0))
        to_mix.append((p, y))
    for item in to_mix:
        to_write.append((item[0], mix(*item)))
    for item in to_write:
        write(*item)


def finish(side, final, lengths, stats, row, weight, latent, lat_rows, edge):
    total, chans, width = row.shape
    frames = total - 2
    lat = latent.shape[0]
    height = lat_rows.shape[1] // lat
    vmem = pl.BlockSpec(memory_space=pltpu.VMEM)
    scratch = [pltpu.VMEM((2, chans, width), F32), pltpu.VMEM((total, chans, width), BF16)]
    if final:
        out = jax.ShapeDtypeStruct((frames, lat, height, width), BF16)
        scratch.append(pltpu.VMEM(lat_rows.shape, F32))
    else:
        out = jax.ShapeDtypeStruct(lat_rows.shape, F32)
    return pl.pallas_call(
        functools.partial(finish_kernel, side, final),
        in_specs=[pl.BlockSpec(memory_space=pltpu.SMEM)] + [vmem] * 6,
        out_specs=vmem,
        out_shape=out,
        scratch_shapes=scratch,
        compiler_params=pltpu.CompilerParams(vmem_limit_bytes=20 * 1024 * 1024),
        cost_estimate=pl.CostEstimate(flops=700_000_000, bytes_accessed=3_000_000, transcendentals=500_000),
    )(lengths, stats, row, weight, latent, lat_rows, edge)


def body(video, cache, conv_weight, latent_weight, clip_lengths):
    _, frames, chans, height, width = video.shape
    video = video.reshape(frames, chans * height, width)
    cache = cache.reshape(2, chans * height, width)
    strips = lax.axis_size("sp")
    first, last, stats = stage(clip_lengths, video, cache, chans, strips)
    stats = lax.all_to_all(stats, "sp", split_axis=0, concat_axis=0, tiled=True)
    first, last, weight = prepare(first, last, conv_weight)
    above = lax.ppermute(last, "sp", [(i, i + 1) for i in range(strips - 1)])
    below = lax.ppermute(first, "sp", [(i + 1, i) for i in range(strips - 1)])
    lat_rows, edge = convolve(clip_lengths, stats, video, cache, weight, latent_weight)
    lat_rows = finish(0, False, clip_lengths, stats, above, weight, latent_weight, lat_rows, edge)
    out = finish(1, True, clip_lengths, stats, below, weight, latent_weight, lat_rows, edge)
    return out[None]


def solution(mesh):
    in_specs = (P("grp", None, None, "sp", None), P("grp", None, None, "sp", None), P(), P(), P())
    out_specs = P("grp", None, None, "sp", None)
    return jax.shard_map(body, mesh=mesh, in_specs=in_specs, out_specs=out_specs, check_vma=False)
```

time: 832 us -> 51.5 us (0.06)
  the two profiles are of different devices: /device:TPU:33 before, /device:TPU:28 now
where the time goes in v1:
time: 51.5 us; the launch traced here: 51.4 us
  Pallas kernels  33.2 us (64%)
  starting transfers between devices  16.2 us (31%)
  waiting for transfers between devices  1.28 us (2%)
  local copies, waits for them, and re-layouts  0.67 us (1%)
    pallas_call x1, Pallas kernels, convolve(): pl.pallas_call(conv_kernel, in_specs=[pl.BlockSpec(memory_space=pltpu.SME...  22.6 us
    all_to_all x1, starting transfers between devices, body(): stats = lax.all_to_all(stats, 'sp', split_axis=0, concat_axis=0, tiled=True)  8.78 us
    pallas_call x2, Pallas kernels, finish(): pl.pallas_call(functools.partial(finish_kernel, side, final), in_specs=[p...  5.54 us
    ppermute x1, starting transfers between devices, body(): below = lax.ppermute(first, 'sp', [(i + 1, i) for i in range(strips - 1)])  5.46 us
    pallas_call x1, Pallas kernels, stage(): pl.pallas_call(stage_kernel, in_specs=[pl.BlockSpec(memory_space=pltpu.SM...  4.83 us
    ppermute x1, starting transfers between devices, body(): above = lax.ppermute(last, 'sp', [(i, i + 1) for i in range(strips - 1)])  1.92 us
    ppermute x1, waiting for transfers between devices, body(): above = lax.ppermute(last, 'sp', [(i, i + 1) for i in range(strips - 1)])  1.28 us
  transfers between devices with their start and end apart: 3, of which 1 were waited for; matrix products, arithmetic and copies ran while one was open for 0% of the time, Pallas kernels for 49%

profile of v1, /device:TPU:28, one launch (start us, length us, event | category | flops | bytes accessed | tf_op | source)
XLA Modules:
  0.0 51.4 jit_solution(38642080622043749)
XLA Ops:
  0.0 0.0 copy-start.1
  0.0 0.7 %copy-done.1 = s32[16]{0:T(128)S(1)} copy-done((s32[16]{0:T(128)S(1)}, s32[16]{0:T(128)}, u32[]{:S(2)}) %copy-start.1) | copy-done | bytes 88
  0.7 0.0 copy-start.3
  0.7 4.8 %shard_map.55 = (bf16[18,128,128]{2,1,0:T(8,128)(2,1)}, bf16[18,128,128]{2,1,0:T(8,128)(2,1)}, f32[16,64]{1,0:T(8,128)}) custom-call(s32[16]{0:T(128)S(1)} %copy-done.1, bf16[16,1024,128]{2,1,0:T(8,128)(2,1)} %bitcast.10, bf16[2,1024,128]{2,1,0:T(8,128)(2,1)} %bitcast.12), custom_call_target="tpu_custom_call" | custom-call | flops 10000000 | bytes 5000000 | tf_op jit(solution)/shard_map/pallas_call | solution.py:87
  5.5 8.8 %all-to-all-start = ((f32[16,1,64]{2,1,0:T(1,128)}), f32[16,1,64]{2,1,0:T(1,128)S(1)}, u32[]{:S(2)}, u32[]{:S(2)}) async-start(f32[16,1,64]{2,1,0:T(1,128)} %bitcast.3), calls=%async_computation | async-start | bytes 16384 | tf_op jit(solution)/shard_map/all_to_all | solution.py:418
  14.3 0.0 copy-done.3
  14.3 0.0 copy-start
  14.3 0.0 copy-start.2
  14.3 0.2 shard_map.56
  14.5 5.5 %collective-permute-start = (bf16[18,128,128]{2,1,0:T(8,128)(2,1)}, bf16[18,128,128]{2,1,0:T(8,128)(2,1)S(1)}, u32[]{:S(2)}, u32[]{:S(2)}) collective-permute-start(bf16[18,128,128]{2,1,0:T(8,128)(2,1)} %get-tuple-element.16), channel_id=1, source_target_pairs={{1,0},{2,1},{3,2},{4,3},{5,4},{6,5},{7,6},{8,7},{9,8},{10,9},{11,1... | collective-permute-start | bytes 1769480 | tf_op jit(solution)/shard_map/ppermute | solution.py:421
  19.9 1.9 %collective-permute-start.1 = (bf16[18,128,128]{2,1,0:T(8,128)(2,1)}, bf16[18,128,128]{2,1,0:T(8,128)(2,1)S(1)}, u32[]{:S(2)}, u32[]{:S(2)}) collective-permute-start(bf16[18,128,128]{2,1,0:T(8,128)(2,1)} %get-tuple-element.18), channel_id=1, source_target_pairs={{0,1},{1,2},{2,3},{3,4},{4,5},{5,6},{6,7},{7,8},{8,9},{9,10},{10,1... | collective-permute-start | bytes 1769480 | tf_op jit(solution)/shard_map/ppermute | solution.py:420
  21.9 0.0 all-to-all-done
  21.9 0.0 copy-done
  21.9 0.0 copy-done.2
  21.9 22.6 %shard_map.57 = (f32[16,128,128]{2,1,0:T(8,128)S(1)}, f32[16,2,128,128]{3,2,1,0:T(8,128)S(1)}) custom-call(s32[16]{0:T(128)S(1)} %copy-done.2, f32[16,64]{1,0:T(8,128)S(1)} %bitcast.7, bf16[16,1024,128]{2,1,0:T(8,128)(2,1)} %bitcast.11, bf16[2,1024,128]{2,1,0:T(8,128)(2,1)} %bitcast.13, bf16[384,1152]{1,0:T(8,128)(2,1)S(1)} %get-tuple-element.17.weight_ref, ...), custom_call_target="tpu_custom_call" | custom-call | flops 12999999488 | bytes 14000000 | tf_op jit(solution)/shard_map/pallas_call | solution.py:305
  44.5 1.3 %collective-permute-done.1.row_ref = bf16[18,128,128]{2,1,0:T(8,128)(2,1)S(1)} collective-permute-done((bf16[18,128,128]{2,1,0:T(8,128)(2,1)}, bf16[18,128,128]{2,1,0:T(8,128)(2,1)S(1)}, u32[]{:S(2)}, u32[]{:S(2)}) %collective-permute-start.1) | collective-permute-done | bytes 589856 | tf_op jit(solution)/shard_map/ppermute | solution.py:420
  45.8 2.4 %shard_map.58.lat_ref = f32[16,128,128]{2,1,0:T(8,128)S(1)} custom-call(s32[16]{0:T(128)S(1)} %copy-done.2, f32[16,64]{1,0:T(8,128)S(1)} %bitcast.8, bf16[18,128,128]{2,1,0:T(8,128)(2,1)S(1)} %collective-permute-done.1.row_ref, bf16[384,1152]{1,0:T(8,128)(2,1)S(1)} %get-tuple-element.17.weight_ref, bf16[16,128]{1,0:T(8,128)(2,1)S(1)} %copy-done, ...), custom_call_target="tpu_custom_call" | custom-call | flops 700000000 | bytes 3000000 | tf_op jit(solution)/shard_map/pallas_call | solution.py:401
  48.2 0.0 collective-permute-done.row_ref
  48.2 3.2 %shard_map.59 = bf16[16,16,8,128]{3,2,1,0:T(8,128)(2,1)} custom-call(s32[16]{0:T(128)S(1)} %copy-done.2, f32[16,64]{1,0:T(8,128)S(1)} %bitcast.9, bf16[18,128,128]{2,1,0:T(8,128)(2,1)S(1)} %collective-permute-done.row_ref, bf16[384,1152]{1,0:T(8,128)(2,1)S(1)} %get-tuple-element.17.weight_ref, bf16[16,128]{1,0:T(8,128)(2,1)S(1)} %copy-done, ...), custom_call_target="tpu_custom_call" | custom-call | flops 700000000 | bytes 3000000 | tf_op jit(solution)/shard_map/pallas_call | solution.py:401
Async XLA Ops:
  0.0 0.7 %copy-start.1 = (s32[16]{0:T(128)S(1)}, s32[16]{0:T(128)}, u32[]{:S(2)}) copy-start(s32[16]{0:T(128)} %lengths_ref.7) | copy-start | bytes 196
  0.7 13.6 %copy-start.3 = (bf16[128,3456]{1,0:T(8,128)(2,1)S(1)}, bf16[128,3456]{1,0:T(8,128)(2,1)}, u32[]{:S(2)}) copy-start(bf16[128,3456]{1,0:T(8,128)(2,1)} %raw_ref.1) | copy-start | bytes 2654212
  5.5 16.4 %all-to-all-start = ((f32[16,1,64]{2,1,0:T(1,128)}), f32[16,1,64]{2,1,0:T(1,128)S(1)}, u32[]{:S(2)}, u32[]{:S(2)}) async-start(f32[16,1,64]{2,1,0:T(1,128)} %bitcast.3), calls=%async_computation | async-start | bytes 16384 | tf_op jit(solution)/shard_map/all_to_all | solution.py:418
  14.3 7.6 %copy-start = (bf16[16,128]{1,0:T(8,128)(2,1)S(1)}, bf16[16,128]{1,0:T(8,128)(2,1)}, u32[]{:S(2)}) copy-start(bf16[16,128]{1,0:T(8,128)(2,1)} %latent_ref.5) | copy-start | bytes 12292
  14.3 7.6 %copy-start.2 = (s32[16]{0:T(128)S(1)}, s32[16]{0:T(128)}, u32[]{:S(2)}) copy-start(s32[16]{0:T(128)} %lengths_ref.7) | copy-start | bytes 196
  14.5 33.7 %collective-permute-start = (bf16[18,128,128]{2,1,0:T(8,128)(2,1)}, bf16[18,128,128]{2,1,0:T(8,128)(2,1)S(1)}, u32[]{:S(2)}, u32[]{:S(2)}) collective-permute-start(bf16[18,128,128]{2,1,0:T(8,128)(2,1)} %get-tuple-element.16), channel_id=1, source_target_pairs={{1,0},{2,1},{3,2},{4,3},{5,4},{6,5},{7,6},{8,7},{9,8},{10,9},{11,1... | collective-permute-start | bytes 1769480 | tf_op jit(solution)/shard_map/ppermute | solution.py:421
  19.9 25.9 %collective-permute-start.1 = (bf16[18,128,128]{2,1,0:T(8,128)(2,1)}, bf16[18,128,128]{2,1,0:T(8,128)(2,1)S(1)}, u32[]{:S(2)}, u32[]{:S(2)}) collective-permute-start(bf16[18,128,128]{2,1,0:T(8,128)(2,1)} %get-tuple-element.18), channel_id=1, source_target_pairs={{0,1},{1,2},{2,3},{3,4},{4,5},{5,6},{6,7},{7,8},{8,9},{9,10},{10,1... | collective-permute-start | bytes 1769480 | tf_op jit(solution)/shard_map/ppermute | solution.py:420
